TPU v7x, 32 devices: a whole 2x2x4 slice. The times are simulated.
32 devices in a mesh: slab: 8 (over y, x, core), img: 4 (over z).
Axes of the slice: x: 2, y: 2, z: 4, core: 2. Of those that a mesh axis runs over, the one named last changes fastest.
Arguments:
- volume: float32 [32, 1024, 1024], P('img', 'slab'), may hold values from -6 to 6
- blk_plane: int32 [128, 8], replicated, may hold values from 0 to 30, all different within a row; in each aligned block of 4 rows (0 to 3, 4 to 7, ...) at most 2 rows name the same one
- blk_row: int32 [128, 8], replicated, may hold values from 0 to 1022
- blk_col: int32 [128, 8], replicated, may hold values from 0 to 7
- frac_plane: float32 [128, 8], replicated, may hold values from 0 to 1
- frac_row: float32 [128, 8], replicated, may hold values from 0 to 1
- defocus: float32 [128], replicated, may hold values from 0.5 to 4
Outputs:
- slices: float32 [128, 8, 2, 128], P(('slab', 'img'))
Inputs may be any that keep to these rules, and one draw needn't show every extreme that they name: `blk_plane`: the blocks of one image name different lower planes. Among the 4 images of one device (aligned groups of images), no plane is the lower plane of more than 2 blocks, and some plane reaches 2.
All inputs are finite; a program needn't handle non-finite values.
Results may differ from a plain program's by a relative error of at most 0.0003.
Values sent between devices are 32-bit elements; how exact they have to be, the bound alone decides.
A program may use at most 128 MiB of HBM per device.

v0:
```python
import functools
import math

import jax
import jax.numpy as jnp
import ml_dtypes
import numpy as np
from jax import lax
from jax.experimental import pallas as pl
from jax.experimental.pallas import tpu as pltpu
from jax.sharding import PartitionSpec as P

LANES = 128
CTF_SCALE = 20.0
CTF_PHASE = 0.07
MOST = 2
MESH = pl.DeviceIdType.MESH
F32 = jnp.float32
BF16 = jnp.bfloat16


def wave_coefficients():
    grid = 0.5 * np.cos(np.linspace(0.0, np.pi, 4001))
    grid = grid[grid > 1e-6]
    basis = (4 * grid * grid)[:, None] ** np.arange(8)
    scale = 4.0 ** np.arange(8)
    cos_c = np.linalg.lstsq(basis, np.cos(2 * np.pi * grid), rcond=None)[0] * scale
    sin_c = np.linalg.lstsq(basis[:, :7] * grid[:, None], np.sin(2 * np.pi * grid), rcond=None)[0] * scale[:7]
    return [float(v) for v in cos_c], [float(v) for v in sin_c]


COS_C, SIN_C = wave_coefficients()


def horner(coefficients, value):
    total = jnp.full_like(value, coefficients[-1])
    for c in coefficients[-2::-1]:
        total = total * value + c
    return total


def wave(turns):
    part = turns - jnp.round(turns)
    square = part * part
    return horner(COS_C, square), part * horner(SIN_C, square)


def split_table(table):
    high = table.astype(ml_dtypes.bfloat16)
    low = (table - high.astype(np.float64)).astype(ml_dtypes.bfloat16)
    return high, low


def column_table(box):
    half = box // 2
    phase = (np.arange(box)[:, None] * np.arange(half)[None, :]) % box
    angle = phase * (2.0 * np.pi / box)
    real, imag = np.cos(angle), -np.sin(angle)
    imag[:, 0] = 1.0 - 2.0 * (np.arange(box) % 2)
    table = np.stack([real.reshape(box, -1, LANES), imag.reshape(box, -1, LANES)], axis=2)
    return split_table(table.reshape(box, box))


def halves(value):
    high = value.astype(BF16)
    low = (value - high.astype(F32)).astype(BF16)
    return high, low


def dot(a, b):
    return jnp.dot(a, b, preferred_element_type=F32)


def kernel(
    dims, meta_ref, vol_hbm, high_hbm, low_hbm, out_ref,
    vol, t_high, t_low, z_high, z_low, g_high, g_low, cols, stage, recv, red, recv2,
    vol_sem, tab_sem, send_sem, recv_sem, send2_sem, recv2_sem,
):
    n_slab, n_img, n_plane, n_row, box, n_group, n_blk, per_step = dims
    n_pair = n_plane + 1
    n_slot = MOST * n_group
    tile = MOST * n_img
    half_blocks = box // LANES // 2
    s, i = lax.axis_index("slab"), lax.axis_index("img")

    tab_copies = [
        pltpu.make_async_copy(high_hbm, t_high, tab_sem.at[0]),
        pltpu.make_async_copy(low_hbm, t_low, tab_sem.at[1]),
    ]

    def vol_copy(q):
        return pltpu.make_async_copy(vol_hbm.at[q], vol.at[q], vol_sem.at[q])

    tab_copies[0].start()
    vol_copy(0).start()
    tab_copies[1].start()
    for q in range(1, n_plane):
        vol_copy(q).start()

    barrier = pltpu.get_barrier_semaphore()
    for d in range(1, n_slab):
        pl.semaphore_signal(barrier, inc=1, device_id=(lax.rem(s + d, n_slab), i), device_id_type=MESH)
    for d in range(1, n_img):
        pl.semaphore_signal(barrier, inc=1, device_id=(s, lax.rem(i + d, n_img)), device_id_type=MESH)

    zero_rows = jnp.zeros((n_row, box), BF16)
    for ref in (z_high, z_low):
        ref[pl.ds(0, n_row)] = zero_rows
        ref[pl.ds((n_plane + 1) * n_row, n_row)] = zero_rows
    red[...] = jnp.zeros_like(red)

    lane = lax.broadcasted_iota(jnp.int32, (1, n_row), 1)
    y = (lane + s * n_row).astype(F32)
    step_cos, step_sin = wave(y * (1.0 / box))
    blk = lax.broadcasted_iota(jnp.int32, (n_slot, n_blk), 1).astype(F32)
    turn = lax.broadcasted_iota(jnp.int32, (n_slot, 1), 0) % MOST

    def weights(pair, carry):
        plane = (n_plane * i - 1 + pair).astype(F32)
        here = meta_ref[0] == plane
        first = jnp.min(jnp.where(here, blk, 1e6), axis=1, keepdims=True)
        last = jnp.max(jnp.where(here, blk, -1.0), axis=1, keepdims=True)
        chosen = jnp.where(turn == 0, first, jnp.where(last > first, last, -2.0))
        mask = blk == chosen

        def pick(k):
            return jnp.sum(jnp.where(mask, meta_ref[k], 0.0), axis=1, keepdims=True)

        row, col, fz, fy = pick(1), pick(2), pick(3), pick(4)
        cols[pair] = jnp.broadcast_to(col, (n_slot, LANES))
        cosine, sine = wave(row * y * (1.0 / box))
        h_real = (1.0 - fy) + fy * step_cos
        h_imag = -fy * step_sin
        g_real = cosine * h_real + sine * h_imag
        g_imag = cosine * h_imag - sine * h_real
        for at, part in ((0, g_real), (n_slot, g_imag)):
            both = jnp.concatenate([part * (1.0 - fz), part * fz], axis=1)
            high, low = halves(both)
            g_high[pair, pl.ds(at, n_slot)] = high
            g_low[pair, pl.ds(at, n_slot)] = low
        return carry

    lax.fori_loop(0, n_pair, weights, 0)

    lane0 = lax.broadcasted_iota(jnp.int32, (n_slot, LANES), 1) == 0

    def evaluate(pair):
        rows = pl.ds(pl.multiple_of(pair * n_row, n_row), 2 * n_row)
        gh, gl = g_high[pair], g_low[pair]
        col = cols[pair]
        mirrored = col >= float(half_blocks)
        wanted = jnp.where(mirrored, 2.0 * half_blocks - 1.0 - col, col)
        wanted = wanted + jnp.where(mirrored & lane0, 1.0, 0.0)
        sign = jnp.where(mirrored, -1.0, 1.0)
        sign = jnp.where(lane0 & (wanted == 0.0), 0.0, sign)
        real = imag = None
        for cb in range(half_blocks):
            at = pl.ds(cb * 2 * LANES, 2 * LANES)
            zh, zl = z_high[rows, at], z_low[rows, at]
            prod = dot(gh, zh) + dot(gl, zh) + dot(gh, zl)
            a, b = prod[:n_slot, :LANES], prod[:n_slot, LANES:]
            c, d = prod[n_slot:, :LANES], prod[n_slot:, LANES:]
            if cb == 0:
                middle = wanted == float(half_blocks)
                real = jnp.where(middle, b, a - sign * d)
                imag = jnp.where(middle, d, c + sign * b)
            else:
                match = wanted == float(cb)
                real = jnp.where(match, a - sign * d, real)
                imag = jnp.where(match, c + sign * b, imag)
        stage[pair, :, pl.ds(0, LANES)] = real
        stage[pair, :, pl.ds(LANES, LANES)] = imag

    def sends(pair):
        copies = []
        for d in range(1, n_slab):
            to = lax.rem(s + d, n_slab)
            copies.append(
                pltpu.make_async_remote_copy(
                    src_ref=stage.at[pair, pl.ds(pl.multiple_of(to * tile, tile), tile)],
                    dst_ref=recv.at[pair, d - 1],
                    send_sem=send_sem.at[pair],
                    recv_sem=recv_sem.at[pair],
                    device_id=(to, i),
                    device_id_type=MESH,
                )
            )
        return copies

    def transform(step):
        for k in range(per_step):
            vol_copy(step * per_step + k).wait()
        x = vol[pl.ds(step * per_step, per_step)].reshape(per_step * n_row, box)
        xh, xl = halves(x)
        rows = pl.ds(pl.multiple_of((step * per_step + 1) * n_row, n_row), per_step * n_row)
        for cb in range(half_blocks):
            at = pl.ds(cb * 2 * LANES, 2 * LANES)
            th, tl = t_high[:, at], t_low[:, at]
            z = dot(xh, th) + dot(xl, th) + dot(xh, tl)
            zh, zl = halves(z)
            z_high[rows, at] = zh
            z_low[rows, at] = zl

    for copy in tab_copies:
        copy.wait()
    pl.semaphore_wait(barrier, n_slab - 1 + n_img - 1)

    def body(step, carry):
        transform(step)
        for k in range(per_step):
            pair = step * per_step + k
            evaluate(pair)
            for copy in sends(pair):
                copy.start()
        return carry

    lax.fori_loop(0, n_plane // per_step, body, 0)
    evaluate(n_plane)
    for copy in sends(n_plane):
        copy.start()

    own = pl.ds(pl.multiple_of(s * tile, tile), tile)
    for pair in range(n_pair):
        pltpu.make_async_copy(recv.at[pair], recv.at[pair], recv_sem.at[pair]).wait()
        total = stage[pair, own]
        for d in range(n_slab - 1):
            total = total + recv[pair, d]
        for to in range(n_img):
            red[to, pl.ds(MOST * pair, MOST)] = total[MOST * to : MOST * to + MOST]

    copies = []
    for d in range(1, n_img):
        to = lax.rem(i + d, n_img)
        copies.append(
            pltpu.make_async_remote_copy(
                src_ref=red.at[to],
                dst_ref=recv2.at[i],
                send_sem=send2_sem.at[d - 1],
                recv_sem=recv2_sem.at[d - 1],
                device_id=(s, to),
                device_id_type=MESH,
            )
        )
    for copy in copies:
        copy.start()
    recv2[i] = red[i]

    group = s * n_img + i
    eye = lax.broadcasted_iota(jnp.int32, (n_blk, n_blk), 0) == lax.broadcasted_iota(jnp.int32, (n_blk, n_blk), 1)
    before = lax.broadcasted_iota(jnp.int32, (n_blk, n_blk), 1) < lax.broadcasted_iota(jnp.int32, (n_blk, n_blk), 0)
    lines = [meta_ref[k, pl.ds(group * MOST, 1)] for k in range(6)]
    plane_b, row_b, col_b, _, _, focus_b = [
        jnp.sum(jnp.where(eye, v, 0.0), axis=1, keepdims=True) for v in lines
    ]
    rank_b = jnp.sum(jnp.where(before & (lines[0] == plane_b), 1.0, 0.0), axis=1, keepdims=True)
    pad = red.shape[1]
    n_sum = n_img * pad
    place = lax.broadcasted_iota(jnp.int32, (n_blk, n_sum), 1)
    img_of = jnp.zeros_like(place)
    for k in range(1, n_img):
        img_of = img_of + jnp.where(place >= k * pad, 1, 0)
    rest = place - img_of * pad
    plane_of = (img_of * n_plane - 1 + rest // MOST).astype(F32)
    turn_of = (rest % MOST).astype(F32)
    take = (rest < MOST * n_pair) & (plane_of == plane_b) & (turn_of == rank_b)
    take = jnp.where(take, 1.0, 0.0).astype(BF16)

    lane_x = lax.broadcasted_iota(jnp.int32, (n_blk, LANES), 1).astype(F32)
    column_x = col_b * LANES + lane_x
    fold_x = jnp.minimum(column_x, box - column_x)
    fold_y = jnp.minimum(row_b, box - row_b)
    wave_sq = (fold_x * fold_x + fold_y * fold_y) * (1.0 / (box * box))
    ctf = -jnp.sin(CTF_SCALE * focus_b * wave_sq + CTF_PHASE) * (1.0 / box)
    turned = (
        lax.broadcasted_iota(jnp.int32, (LANES, LANES), 0) + lax.broadcasted_iota(jnp.int32, (LANES, LANES), 1)
    ) % LANES == 0
    turned = jnp.where(turned, 1.0, 0.0).astype(BF16)
    mirrored_b = col_b >= float(half_blocks)

    for copy in copies:
        copy.wait_recv()
    all_high, all_low = halves(recv2[...].reshape(n_sum, 2 * LANES))
    value = dot(take, all_high) + dot(take, all_low)
    for k in range(2):
        part = value[:, k * LANES : (k + 1) * LANES]
        high, low = halves(part)
        back = dot(high, turned) + dot(low, turned)
        out_ref[:, k, :] = jnp.where(mirrored_b, back, part) * ctf

    for copy in copies:
        copy.wait_send()
    for pair in range(n_pair):
        some = stage.at[pair, pl.ds(0, (n_slab - 1) * tile)]
        pltpu.make_async_copy(some, some, send_sem.at[pair]).wait()


def on_device(n_slab, n_img, volume, blk_plane, blk_row, blk_col, frac_plane, frac_row, defocus):
    n_plane, n_row, box = volume.shape
    n_image, img_blk = blk_plane.shape
    n_group = n_slab * n_img
    n_blk = n_image // n_group * img_blk
    n_pair = n_plane + 1
    n_slot = MOST * n_group
    tile = MOST * n_img
    per_step = 2
    pad = -(-MOST * n_pair // 8) * 8
    focus = jnp.broadcast_to(defocus[:, None], blk_plane.shape)
    meta = jnp.stack(
        [v.astype(F32) for v in (blk_plane, blk_row, blk_col, frac_plane, frac_row, focus)]
    ).reshape(6, n_group, 1, n_blk)
    meta = jnp.broadcast_to(meta, (6, n_group, MOST, n_blk)).reshape(6, n_slot, n_blk)
    table_high, table_low = column_table(box)
    dims = (n_slab, n_img, n_plane, n_row, box, n_group, n_blk, per_step)
    any_space = pl.BlockSpec(memory_space=pl.ANY)
    vmem = pl.BlockSpec(memory_space=pltpu.VMEM)
    out = pl.pallas_call(
        functools.partial(kernel, dims),
        out_shape=jax.ShapeDtypeStruct((n_blk, 2, LANES), F32),
        in_specs=[vmem, any_space, any_space, any_space],
        out_specs=vmem,
        scratch_shapes=[
            pltpu.VMEM((n_plane, n_row, box), F32),
            pltpu.VMEM((box, box), BF16),
            pltpu.VMEM((box, box), BF16),
            pltpu.VMEM(((n_plane + 2) * n_row, box), BF16),
            pltpu.VMEM(((n_plane + 2) * n_row, box), BF16),
            pltpu.VMEM((n_pair, 2 * n_slot, 2 * n_row), BF16),
            pltpu.VMEM((n_pair, 2 * n_slot, 2 * n_row), BF16),
            pltpu.VMEM((n_pair, n_slot, LANES), F32),
            pltpu.VMEM((n_pair, n_slot, 2 * LANES), F32),
            pltpu.VMEM((n_pair, n_slab - 1, tile, 2 * LANES), F32),
            pltpu.VMEM((n_img, pad, 2 * LANES), F32),
            pltpu.VMEM((n_img, pad, 2 * LANES), F32),
            pltpu.SemaphoreType.DMA((n_plane,)),
            pltpu.SemaphoreType.DMA((2,)),
            pltpu.SemaphoreType.DMA((n_pair,)),
            pltpu.SemaphoreType.DMA((n_pair,)),
            pltpu.SemaphoreType.DMA((n_img - 1,)),
            pltpu.SemaphoreType.DMA((n_img - 1,)),
        ],
        compiler_params=pltpu.CompilerParams(
            collective_id=0, has_side_effects=True, vmem_limit_bytes=58 * 1024 * 1024
        ),
        cost_estimate=pl.CostEstimate(flops=8_000_000_000, bytes_accessed=9_000_000, transcendentals=0),
        name="slices",
    )(meta, volume, jnp.asarray(table_high), jnp.asarray(table_low))
    return out.reshape(n_image // n_group, img_blk, 2, LANES)


def solution(mesh):
    placed = (P("img", "slab", None), P(), P(), P(), P(), P(), P())
    return jax.shard_map(
        functools.partial(on_device, mesh.shape["slab"], mesh.shape["img"]),
        mesh=mesh,
        in_specs=placed,
        out_specs=P(("slab", "img"), None, None, None),
        check_vma=False,
    )
```

profile of v0, /device:TPU:0, one launch (start us, length us, event | category | flops | bytes accessed | tf_op | source)
XLA Modules:
  0.0 35.4 jit_solution(16271421066072415602)
XLA Ops:
  0.0 0.7 %convert_element_type.9 = f32[128,8]{0,1:T(8,128)S(1)} convert(s32[128,8]{0,1:T(8,128)} %param.10) | non-fusion elementwise | flops 1024 | bytes 8192 | tf_op jit(solution)/shard_map/convert_element_type | solution.py:309
  0.7 0.7 %convert_element_type.10 = f32[128,8]{0,1:T(8,128)S(1)} convert(s32[128,8]{0,1:T(8,128)} %param.11) | non-fusion elementwise | flops 1024 | bytes 8192 | tf_op jit(solution)/shard_map/convert_element_type | solution.py:309
  1.4 0.7 %convert_element_type.11 = f32[128,8]{0,1:T(8,128)S(1)} convert(s32[128,8]{0,1:T(8,128)} %param.12) | non-fusion elementwise | flops 1024 | bytes 8192 | tf_op jit(solution)/shard_map/convert_element_type | solution.py:309
  2.1 0.7 %stack_broadcast_in_dim.9 = f32[32,4]{1,0:T(8,128)S(1)} reshape(f32[128]{0:T(128)} %param.15) | data formatting | bytes 1024 | tf_op jit(solution)/shard_map/stack;broadcast_in_dim | solution.py:308
  2.8 0.1 copy.15
  2.9 0.1 copy.16
  3.0 0.1 copy.12
  3.1 0.1 stack.20
  3.2 0.1 copy.11
  3.3 0.1 stack.19
  3.4 0.1 copy.10
  3.5 0.1 stack.18
  3.5 0.8 %copy.13 = f32[128,8]{1,0:T(8,128)S(1)} copy(f32[128,8]{0,1:T(8,128)} %param.13) | data formatting | bytes 8192 | tf_op args[4]
  4.3 0.1 stack.21
  4.4 0.8 %copy.14 = f32[128,8]{1,0:T(8,128)S(1)} copy(f32[128,8]{0,1:T(8,128)} %param.14) | data formatting | bytes 8192 | tf_op args[5]
  5.2 0.1 stack.22
  5.4 0.7 %broadcast_in_dim.9 = f32[6,32,2,32]{3,2,1,0:T(2,128)} broadcast(f32[6,32,32]{2,1,0:T(8,128)S(1)} %bitcast.6), dimensions={0,1,3} | broadcast | bytes 73728 | tf_op jit(solution)/shard_map/broadcast_in_dim | solution.py:311
  6.1 27.9 %slices.1 = f32[32,2,128]{2,1,0:T(2,128)} custom-call(f32[6,64,32]{2,1,0:T(8,128)} %bitcast.5, f32[8,128,1024]{2,1,0:T(8,128)} %vol_hbm.1, bf16[1024,1024]{1,0:T(8,128)(2,1)} %constant.4.clone.high_hbm, bf16[1024,1024]{1,0:T(8,128)(2,1)} %constant.5.clone.low_hbm), custom_call_target="tpu_custom_call" | custom-call | flops 8000000000 | bytes 9000000 | tf_op jit(solution)/shard_map/slices/pallas_call | solution.py:316
  34.0 1.4 %copy.23 = f32[4,8,2,128]{3,2,1,0:T(2,128)} copy(f32[4,8,2,128]{3,2,1,0:T(2,128)} %bitcast.7) | data formatting | bytes 65536
  (7 shorter events, 0.0 us)
where the time goes:
time: 35.7 us; the launch traced here: 35.4 us
  Pallas kernels  27.9 us (78%)
  local copies, waits for them, and re-layouts  5.33 us (15%)
  other arithmetic  2.07 us (6%)
    pallas_call x1, Pallas kernels, on_device(): pl.pallas_call(functools.partial(kernel, dims), out_shape=jax.ShapeDtypeS...  27.9 us
    unnamed x8, local copies, waits for them, and re-layouts  2.98 us
    convert_element_type x3, other arithmetic, on_device(): v.astype(F32)  2.07 us
    another operation x10, local copies, waits for them, and re-layouts, on_device(): jnp.stack([v.astype(F32) for v in (blk_plane, blk_row, blk_col, frac_plan...  1.3 us
    broadcast_in_dim x1, local copies, waits for them, and re-layouts, on_device(): jnp.broadcast_to(meta, (6, n_group, MOST, n_blk)).reshape(6, n_slot, n_blk)  0.74 us

commit v1 on v0

--- a/solution.py
+++ b/solution.py
@@ -52,13 +52,19 @@
 
 
 def column_table(box):
-    half = box // 2
-    phase = (np.arange(box)[:, None] * np.arange(half)[None, :]) % box
-    angle = phase * (2.0 * np.pi / box)
-    real, imag = np.cos(angle), -np.sin(angle)
-    imag[:, 0] = 1.0 - 2.0 * (np.arange(box) % 2)
-    table = np.stack([real.reshape(box, -1, LANES), imag.reshape(box, -1, LANES)], axis=2)
-    return split_table(table.reshape(box, box))
+    half, lower = box // 2, LANES // 2
+    lane = np.arange(LANES)
+    parts = []
+    for u in range(half // LANES // 2):
+        first = 2 * u * LANES
+        even = first + 2 * lane
+        odd = first + np.where(lane < lower, LANES + 2 * lane + 1, 2 * (lane - lower) + 1)
+        for wanted in (even, odd):
+            angle = ((np.arange(half)[:, None] * wanted[None, :]) % box) * (2.0 * np.pi / box)
+            real, imag = np.cos(angle), -np.sin(angle)
+            imag[:, wanted == 0] = (1.0 - 2.0 * (np.arange(half) % 2))[:, None]
+            parts += [real, imag]
+    return split_table(np.concatenate(parts, axis=1))
 
 
 def halves(value):
@@ -72,17 +78,27 @@
 
 
 def kernel(
-    dims, meta_ref, vol_hbm, high_hbm, low_hbm, out_ref,
-    vol, t_high, t_low, z_high, z_low, g_high, g_low, cols, stage, recv, red, recv2,
-    vol_sem, tab_sem, send_sem, recv_sem, send2_sem, recv2_sem,
+    dims, plane_hbm, row_hbm, col_hbm, fz_hbm, fy_hbm, focus_hbm, vol_hbm, high_hbm, low_hbm, out_ref,
+    ints, floats, focus_ref, meta_ref, vol, t_high, t_low, z_high, z_low, stage, recv, red, recv2,
+    meta_sem, vol_sem, tab_sem, send_sem, recv_sem, send2_sem, recv2_sem,
 ):
     n_slab, n_img, n_plane, n_row, box, n_group, n_blk, per_step = dims
     n_pair = n_plane + 1
     n_slot = MOST * n_group
     tile = MOST * n_img
     half_blocks = box // LANES // 2
+    lower = LANES // 2
     s, i = lax.axis_index("slab"), lax.axis_index("img")
 
+    meta_copies = [
+        pltpu.make_async_copy(source, target, meta_sem.at[k])
+        for k, (source, target) in enumerate(
+            [
+                (plane_hbm, ints.at[0]), (row_hbm, ints.at[1]), (col_hbm, ints.at[2]),
+                (fz_hbm, floats.at[0]), (fy_hbm, floats.at[1]), (focus_hbm, focus_ref),
+            ]
+        )
+    ]
     tab_copies = [
         pltpu.make_async_copy(high_hbm, t_high, tab_sem.at[0]),
         pltpu.make_async_copy(low_hbm, t_low, tab_sem.at[1]),
@@ -91,10 +107,13 @@
     def vol_copy(q):
         return pltpu.make_async_copy(vol_hbm.at[q], vol.at[q], vol_sem.at[q])
 
+    for copy in meta_copies:
+        copy.start()
     tab_copies[0].start()
-    vol_copy(0).start()
+    for q in range(per_step):
+        vol_copy(q).start()
     tab_copies[1].start()
-    for q in range(1, n_plane):
+    for q in range(per_step, n_plane):
         vol_copy(q).start()
 
     barrier = pltpu.get_barrier_semaphore()
@@ -109,13 +128,32 @@
         ref[pl.ds((n_plane + 1) * n_row, n_row)] = zero_rows
     red[...] = jnp.zeros_like(red)
 
+    for copy in meta_copies:
+        copy.wait()
+    img_blk, n_image = ints.shape[1:]
+    own_images = n_image // n_group
+    image = lax.broadcasted_iota(jnp.int32, (n_blk, n_image), 1)
+    within = lax.broadcasted_iota(jnp.int32, (n_blk, n_image), 0) // img_blk
+    in_turn = image % own_images == within
+    slot_at = lax.broadcasted_iota(jnp.int32, (n_slot, n_image), 0) // MOST
+    image_at = lax.broadcasted_iota(jnp.int32, (n_slot, n_image), 1) // own_images
+    spread = jnp.where(slot_at == image_at, 1.0, 0.0)
+    sources = [ints[k].astype(F32) for k in range(3)] + [floats[0], floats[1]]
+    sources.append(jnp.broadcast_to(focus_ref[...], (img_blk, n_image)))
+    for k, source in enumerate(sources):
+        laid = jnp.where(in_turn, jnp.concatenate([source] * own_images, axis=0), 0.0)
+        meta_ref[k] = lax.dot_general(
+            spread, laid, (((1,), (1,)), ((), ())),
+            precision=lax.Precision.HIGHEST, preferred_element_type=F32,
+        )
+
     lane = lax.broadcasted_iota(jnp.int32, (1, n_row), 1)
     y = (lane + s * n_row).astype(F32)
     step_cos, step_sin = wave(y * (1.0 / box))
     blk = lax.broadcasted_iota(jnp.int32, (n_slot, n_blk), 1).astype(F32)
     turn = lax.broadcasted_iota(jnp.int32, (n_slot, 1), 0) % MOST
 
-    def weights(pair, carry):
+    def weights(pair):
         plane = (n_plane * i - 1 + pair).astype(F32)
         here = meta_ref[0] == plane
         first = jnp.min(jnp.where(here, blk, 1e6), axis=1, keepdims=True)
@@ -127,49 +165,54 @@
             return jnp.sum(jnp.where(mask, meta_ref[k], 0.0), axis=1, keepdims=True)
 
         row, col, fz, fy = pick(1), pick(2), pick(3), pick(4)
-        cols[pair] = jnp.broadcast_to(col, (n_slot, LANES))
         cosine, sine = wave(row * y * (1.0 / box))
         h_real = (1.0 - fy) + fy * step_cos
         h_imag = -fy * step_sin
         g_real = cosine * h_real + sine * h_imag
         g_imag = cosine * h_imag - sine * h_real
-        for at, part in ((0, g_real), (n_slot, g_imag)):
-            both = jnp.concatenate([part * (1.0 - fz), part * fz], axis=1)
-            high, low = halves(both)
-            g_high[pair, pl.ds(at, n_slot)] = high
-            g_low[pair, pl.ds(at, n_slot)] = low
-        return carry
-
-    lax.fori_loop(0, n_pair, weights, 0)
-
-    lane0 = lax.broadcasted_iota(jnp.int32, (n_slot, LANES), 1) == 0
-
-    def evaluate(pair):
-        rows = pl.ds(pl.multiple_of(pair * n_row, n_row), 2 * n_row)
-        gh, gl = g_high[pair], g_low[pair]
-        col = cols[pair]
+        both = [jnp.concatenate([part * (1.0 - fz), part * fz], axis=1) for part in (g_real, g_imag)]
+        high, low = halves(jnp.concatenate(both, axis=0))
+        return col, high, low
+
+    slot_lane = lax.broadcasted_iota(jnp.int32, (n_slot, LANES), 1)
+
+    def evaluate(pair, given):
+        rows = pl.ds(pair * n_row, 2 * n_row)
+        if not isinstance(pair, int):
+            rows = pl.ds(pl.multiple_of(pair * n_row, n_row), 2 * n_row)
+        col, gh, gl = given
         mirrored = col >= float(half_blocks)
-        wanted = jnp.where(mirrored, 2.0 * half_blocks - 1.0 - col, col)
-        wanted = wanted + jnp.where(mirrored & lane0, 1.0, 0.0)
+        base = jnp.where(mirrored, 2.0 * half_blocks - 1.0 - col, col)
+        odd = base - 2.0 * jnp.floor(base * 0.5)
+        wanted = jnp.where(slot_lane < lower, base, base + 1.0 - 2.0 * odd)
         sign = jnp.where(mirrored, -1.0, 1.0)
-        sign = jnp.where(lane0 & (wanted == 0.0), 0.0, sign)
-        real = imag = None
+        sign = jnp.where((slot_lane == 0) & (wanted == 0.0), 0.0, sign)
+        beyond = jnp.where(base == half_blocks - 1.0, -1.0, base + odd)
+        beyond = jnp.broadcast_to(beyond, (n_slot, LANES))
+        real = imag = past_real = past_imag = None
         for cb in range(half_blocks):
             at = pl.ds(cb * 2 * LANES, 2 * LANES)
             zh, zl = z_high[rows, at], z_low[rows, at]
             prod = dot(gh, zh) + dot(gl, zh) + dot(gh, zl)
             a, b = prod[:n_slot, :LANES], prod[:n_slot, LANES:]
             c, d = prod[n_slot:, :LANES], prod[n_slot:, LANES:]
+            now_real, now_imag = a - sign * d, c + sign * b
             if cb == 0:
-                middle = wanted == float(half_blocks)
-                real = jnp.where(middle, b, a - sign * d)
-                imag = jnp.where(middle, d, c + sign * b)
+                real, imag = now_real, now_imag
+                middle = beyond == -1.0
+                past_real = jnp.where(middle, b, now_real)
+                past_imag = jnp.where(middle, d, now_imag)
             else:
                 match = wanted == float(cb)
-                real = jnp.where(match, a - sign * d, real)
-                imag = jnp.where(match, c + sign * b, imag)
-        stage[pair, :, pl.ds(0, LANES)] = real
-        stage[pair, :, pl.ds(LANES, LANES)] = imag
+                real = jnp.where(match, now_real, real)
+                imag = jnp.where(match, now_imag, imag)
+                if cb % 2 == 0:
+                    match = beyond == float(cb)
+                    past_real = jnp.where(match, now_real, past_real)
+                    past_imag = jnp.where(match, now_imag, past_imag)
+        put = mirrored & (slot_lane == jnp.where(odd > 0.0, lower, 0))
+        stage[pair, :, pl.ds(0, LANES)] = jnp.where(put, pltpu.roll(past_real, lower, 1), real)
+        stage[pair, :, pl.ds(LANES, LANES)] = jnp.where(put, pltpu.roll(past_imag, lower, 1), imag)
 
     def sends(pair):
         copies = []
@@ -190,10 +233,16 @@
     def transform(step):
         for k in range(per_step):
             vol_copy(step * per_step + k).wait()
-        x = vol[pl.ds(step * per_step, per_step)].reshape(per_step * n_row, box)
-        xh, xl = halves(x)
-        rows = pl.ds(pl.multiple_of((step * per_step + 1) * n_row, n_row), per_step * n_row)
+        planes = pl.ds(step * per_step, per_step)
+        near = vol[planes, :, pl.ds(0, box // 2)].reshape(per_step * n_row, box // 2)
+        far = vol[planes, :, pl.ds(box // 2, box // 2)].reshape(per_step * n_row, box // 2)
+        inputs = (halves(near + far), halves(near - far))
+        if step == 0:
+            for copy in tab_copies:
+                copy.wait()
+        rows = pl.ds((step * per_step + 1) * n_row, per_step * n_row)
         for cb in range(half_blocks):
+            xh, xl = inputs[cb % 2]
             at = pl.ds(cb * 2 * LANES, 2 * LANES)
             th, tl = t_high[:, at], t_low[:, at]
             z = dot(xh, th) + dot(xl, th) + dot(xh, tl)
@@ -201,21 +250,30 @@
             z_high[rows, at] = zh
             z_low[rows, at] = zl
 
-    for copy in tab_copies:
-        copy.wait()
-    pl.semaphore_wait(barrier, n_slab - 1 + n_img - 1)
-
-    def body(step, carry):
-        transform(step)
-        for k in range(per_step):
-            pair = step * per_step + k
-            evaluate(pair)
-            for copy in sends(pair):
-                copy.start()
-        return carry
-
-    lax.fori_loop(0, n_plane // per_step, body, 0)
-    evaluate(n_plane)
+    for step in range(n_plane // per_step):
+        if per_step <= 2:
+            given = [weights(step * per_step + k) for k in range(per_step)]
+            transform(step)
+            if step == 0:
+                pl.semaphore_wait(barrier, n_slab - 1 + n_img - 1)
+            for k in range(per_step):
+                pair = step * per_step + k
+                evaluate(pair, given[k])
+                for copy in sends(pair):
+                    copy.start()
+        else:
+            transform(step)
+            if step == 0:
+                pl.semaphore_wait(barrier, n_slab - 1 + n_img - 1)
+
+            def body(k, carry):
+                evaluate(k, weights(k))
+                for copy in sends(k):
+                    copy.start()
+                return carry
+
+            lax.fori_loop(step * per_step, (step + 1) * per_step, body, 0)
+    evaluate(n_plane, weights(n_plane))
     for copy in sends(n_plane):
         copy.start()
 
@@ -271,11 +329,20 @@
     fold_y = jnp.minimum(row_b, box - row_b)
     wave_sq = (fold_x * fold_x + fold_y * fold_y) * (1.0 / (box * box))
     ctf = -jnp.sin(CTF_SCALE * focus_b * wave_sq + CTF_PHASE) * (1.0 / box)
-    turned = (
-        lax.broadcasted_iota(jnp.int32, (LANES, LANES), 0) + lax.broadcasted_iota(jnp.int32, (LANES, LANES), 1)
-    ) % LANES == 0
-    turned = jnp.where(turned, 1.0, 0.0).astype(BF16)
+    source_lane = lax.broadcasted_iota(jnp.int32, (LANES, LANES), 0)
+    target_lane = lax.broadcasted_iota(jnp.int32, (LANES, LANES), 1)
+    low_half = source_lane < lower
+    orders = []
+    for offset in (
+        jnp.where(low_half, 2 * source_lane, 2 * source_lane - LANES + 1),
+        jnp.where(low_half, 2 * source_lane + 1, 2 * source_lane - LANES),
+    ):
+        orders.append(offset == target_lane)
+        orders.append((offset + target_lane) % LANES == 0)
+    orders = jnp.concatenate([jnp.where(v, 1.0, 0.0).astype(BF16) for v in orders], axis=1)
     mirrored_b = col_b >= float(half_blocks)
+    base_b = jnp.where(mirrored_b, 2.0 * half_blocks - 1.0 - col_b, col_b)
+    odd_b = base_b - 2.0 * jnp.floor(base_b * 0.5) > 0.0
 
     for copy in copies:
         copy.wait_recv()
@@ -284,8 +351,11 @@
     for k in range(2):
         part = value[:, k * LANES : (k + 1) * LANES]
         high, low = halves(part)
-        back = dot(high, turned) + dot(low, turned)
-        out_ref[:, k, :] = jnp.where(mirrored_b, back, part) * ctf
+        laid = dot(high, orders) + dot(low, orders)
+        laid = [laid[:, v * LANES : (v + 1) * LANES] for v in range(4)]
+        even = jnp.where(mirrored_b, laid[1], laid[0])
+        odd = jnp.where(mirrored_b, laid[3], laid[2])
+        out_ref[:, k, :] = jnp.where(odd_b, odd, even) * ctf
 
     for copy in copies:
         copy.wait_send()
@@ -302,13 +372,8 @@
     n_pair = n_plane + 1
     n_slot = MOST * n_group
     tile = MOST * n_img
-    per_step = 2
+    per_step = max(1, min(n_plane, 256 // n_row))
     pad = -(-MOST * n_pair // 8) * 8
-    focus = jnp.broadcast_to(defocus[:, None], blk_plane.shape)
-    meta = jnp.stack(
-        [v.astype(F32) for v in (blk_plane, blk_row, blk_col, frac_plane, frac_row, focus)]
-    ).reshape(6, n_group, 1, n_blk)
-    meta = jnp.broadcast_to(meta, (6, n_group, MOST, n_blk)).reshape(6, n_slot, n_blk)
     table_high, table_low = column_table(box)
     dims = (n_slab, n_img, n_plane, n_row, box, n_group, n_blk, per_step)
     any_space = pl.BlockSpec(memory_space=pl.ANY)
@@ -316,21 +381,23 @@
     out = pl.pallas_call(
         functools.partial(kernel, dims),
         out_shape=jax.ShapeDtypeStruct((n_blk, 2, LANES), F32),
-        in_specs=[vmem, any_space, any_space, any_space],
+        in_specs=[any_space] * 9,
         out_specs=vmem,
         scratch_shapes=[
+            pltpu.VMEM((3, img_blk, n_image), jnp.int32),
+            pltpu.VMEM((2, img_blk, n_image), F32),
+            pltpu.VMEM((1, n_image), F32),
+            pltpu.VMEM((6, n_slot, n_blk), F32),
             pltpu.VMEM((n_plane, n_row, box), F32),
-            pltpu.VMEM((box, box), BF16),
-            pltpu.VMEM((box, box), BF16),
+            pltpu.VMEM((box // 2, box), BF16),
+            pltpu.VMEM((box // 2, box), BF16),
             pltpu.VMEM(((n_plane + 2) * n_row, box), BF16),
             pltpu.VMEM(((n_plane + 2) * n_row, box), BF16),
-            pltpu.VMEM((n_pair, 2 * n_slot, 2 * n_row), BF16),
-            pltpu.VMEM((n_pair, 2 * n_slot, 2 * n_row), BF16),
-            pltpu.VMEM((n_pair, n_slot, LANES), F32),
             pltpu.VMEM((n_pair, n_slot, 2 * LANES), F32),
             pltpu.VMEM((n_pair, n_slab - 1, tile, 2 * LANES), F32),
             pltpu.VMEM((n_img, pad, 2 * LANES), F32),
             pltpu.VMEM((n_img, pad, 2 * LANES), F32),
+            pltpu.SemaphoreType.DMA((6,)),
             pltpu.SemaphoreType.DMA((n_plane,)),
             pltpu.SemaphoreType.DMA((2,)),
             pltpu.SemaphoreType.DMA((n_pair,)),
@@ -343,7 +410,10 @@
         ),
         cost_estimate=pl.CostEstimate(flops=8_000_000_000, bytes_accessed=9_000_000, transcendentals=0),
         name="slices",
-    )(meta, volume, jnp.asarray(table_high), jnp.asarray(table_low))
+    )(
+        blk_plane.T, blk_row.T, blk_col.T, frac_plane.T, frac_row.T, defocus[None, :],
+        volume, jnp.asarray(table_high), jnp.asarray(table_low),
+    )
     return out.reshape(n_image // n_group, img_blk, 2, LANES)
 
 

time: 35.7 us -> 24.9 us (0.70)
  Pallas kernels: 27.9 us -> 23.3 us
  local copies, waits for them, and re-layouts: 5.33 us -> 1.38 us
  other arithmetic: 2.07 us -> 0 us
    pallas_call x1, Pallas kernels: 27.9 us -> 23.3 us  [on_device(): pl.pallas_call(functools.partial(kernel, dims), out_shape=jax.ShapeDtypeS...]
    convert_element_type x3 -> x0, other arithmetic: 2.07 us -> none  [on_device(): v.astype(F32)]
    unnamed x8 -> x1, local copies, waits for them, and re-layouts: 2.98 us -> 1.38 us
    another operation x10 -> x0, local copies, waits for them, and re-layouts: 1.3 us -> none  [on_device(): jnp.stack([v.astype(F32) for v in (blk_plane, blk_row, blk_col, frac_plan...]
    broadcast_in_dim x1 -> x0, local copies, waits for them, and re-layouts: 0.74 us -> none  [on_device(): jnp.broadcast_to(meta, (6, n_group, MOST, n_blk)).reshape(6, n_slot, n_blk)]
where the time goes in v1:
time: 24.9 us; the launch traced here: 24.7 us
  Pallas kernels  23.3 us (94%)
  local copies, waits for them, and re-layouts  1.38 us (6%)
    pallas_call x1, Pallas kernels, on_device(): pl.pallas_call(functools.partial(kernel, dims), out_shape=jax.ShapeDtypeS...  23.3 us
    unnamed x1, local copies, waits for them, and re-layouts  1.38 us

profile of v1, /device:TPU:0, one launch (start us, length us, event | category | flops | bytes accessed | tf_op | source)
XLA Modules:
  0.0 24.7 jit_solution(13144387024977843875)
XLA Ops:
  0.0 23.3 %slices.1 = f32[32,2,128]{2,1,0:T(2,128)} custom-call(s32[8,128]{1,0:T(8,128)} %bitcast.8, s32[8,128]{1,0:T(8,128)} %bitcast.9, s32[8,128]{1,0:T(8,128)} %bitcast.10, f32[8,128]{1,0:T(8,128)} %bitcast.11, f32[8,128]{1,0:T(8,128)} %bitcast.12, f32[1,128]{1,0:T(1,128)} %bitcast.13, f32[8,128,1024]{2,1,0:T(8,128)} %vol_hbm.1, ...), custom_call_target="tpu_custom_call" | custom-call | flops 8000000000 | bytes 9000000 | tf_op jit(solution)/shard_map/slices/pallas_call | solution.py:381
  23.3 1.4 %copy.11 = f32[4,8,2,128]{3,2,1,0:T(2,128)} copy(f32[4,8,2,128]{3,2,1,0:T(2,128)} %bitcast.7) | data formatting | bytes 65536

commit v2 on v1

--- a/solution.py
+++ b/solution.py
@@ -14,6 +14,7 @@
 CTF_SCALE = 20.0
 CTF_PHASE = 0.07
 MOST = 2
+CORES = 2
 MESH = pl.DeviceIdType.MESH
 F32 = jnp.float32
 BF16 = jnp.bfloat16
@@ -79,8 +80,8 @@
 
 def kernel(
     dims, plane_hbm, row_hbm, col_hbm, fz_hbm, fy_hbm, focus_hbm, vol_hbm, high_hbm, low_hbm, out_ref,
-    ints, floats, focus_ref, meta_ref, vol, t_high, t_low, z_high, z_low, stage, recv, red, recv2,
-    meta_sem, vol_sem, tab_sem, send_sem, recv_sem, send2_sem, recv2_sem,
+    ints, floats, focus_ref, meta_ref, vol, t_high, t_low, z_high, z_low, stage, recv_twin, joined, recv, red, recv2,
+    meta_sem, vol_sem, tab_sem, twin_sem, send_sem, recv_sem, send2_sem, recv2_sem,
 ):
     n_slab, n_img, n_plane, n_row, box, n_group, n_blk, per_step = dims
     n_pair = n_plane + 1
@@ -88,7 +89,11 @@
     tile = MOST * n_img
     half_blocks = box // LANES // 2
     lower = LANES // 2
+    n_chip = n_slab // CORES
+    half_slots = n_slot // CORES
     s, i = lax.axis_index("slab"), lax.axis_index("img")
+    chip, core = s // CORES, s % CORES
+    twin = chip * CORES + 1 - core
 
     meta_copies = [
         pltpu.make_async_copy(source, target, meta_sem.at[k])
@@ -117,8 +122,10 @@
         vol_copy(q).start()
 
     barrier = pltpu.get_barrier_semaphore()
-    for d in range(1, n_slab):
-        pl.semaphore_signal(barrier, inc=1, device_id=(lax.rem(s + d, n_slab), i), device_id_type=MESH)
+    pl.semaphore_signal(barrier, inc=1, device_id=(twin, i), device_id_type=MESH)
+    for d in range(1, n_chip):
+        to = lax.rem(chip + d, n_chip) * CORES + core
+        pl.semaphore_signal(barrier, inc=1, device_id=(to, i), device_id_type=MESH)
     for d in range(1, n_img):
         pl.semaphore_signal(barrier, inc=1, device_id=(s, lax.rem(i + d, n_img)), device_id_type=MESH)
 
@@ -135,7 +142,10 @@
     image = lax.broadcasted_iota(jnp.int32, (n_blk, n_image), 1)
     within = lax.broadcasted_iota(jnp.int32, (n_blk, n_image), 0) // img_blk
     in_turn = image % own_images == within
-    slot_at = lax.broadcasted_iota(jnp.int32, (n_slot, n_image), 0) // MOST
+    slot_at = lax.broadcasted_iota(jnp.int32, (n_slot, n_image), 0)
+    slot_core = jnp.where(slot_at >= half_slots, 1, 0)
+    slot_at = slot_at - slot_core * half_slots
+    slot_at = (slot_at // tile * CORES + slot_core) * n_img + slot_at % tile // MOST
     image_at = lax.broadcasted_iota(jnp.int32, (n_slot, n_image), 1) // own_images
     spread = jnp.where(slot_at == image_at, 1.0, 0.0)
     sources = [ints[k].astype(F32) for k in range(3)] + [floats[0], floats[1]]
@@ -214,34 +224,58 @@
         stage[pair, :, pl.ds(0, LANES)] = jnp.where(put, pltpu.roll(past_real, lower, 1), real)
         stage[pair, :, pl.ds(LANES, LANES)] = jnp.where(put, pltpu.roll(past_imag, lower, 1), imag)
 
-    def sends(pair):
+    n_step = n_plane // per_step
+    spans = [(g * per_step, per_step) for g in range(n_step)]
+    spans[-1] = (spans[-1][0], per_step + 1)
+    own_half = pl.multiple_of(core * half_slots, half_slots)
+    other_half = pl.multiple_of((1 - core) * half_slots, half_slots)
+
+    def twin_copy(g):
+        pairs = pl.ds(*spans[g])
+        return pltpu.make_async_remote_copy(
+            src_ref=stage.at[pairs, pl.ds(other_half, half_slots)],
+            dst_ref=recv_twin.at[pairs],
+            send_sem=twin_sem.at[0, g],
+            recv_sem=twin_sem.at[1, g],
+            device_id=(twin, i),
+            device_id_type=MESH,
+        )
+
+    def chip_copies(g):
+        pairs = pl.ds(*spans[g])
         copies = []
-        for d in range(1, n_slab):
-            to = lax.rem(s + d, n_slab)
+        for d in range(1, n_chip):
+            to = lax.rem(chip + d, n_chip)
             copies.append(
                 pltpu.make_async_remote_copy(
-                    src_ref=stage.at[pair, pl.ds(pl.multiple_of(to * tile, tile), tile)],
-                    dst_ref=recv.at[pair, d - 1],
-                    send_sem=send_sem.at[pair],
-                    recv_sem=recv_sem.at[pair],
-                    device_id=(to, i),
+                    src_ref=joined.at[pairs, pl.ds(pl.multiple_of(to * tile, tile), tile)],
+                    dst_ref=recv.at[d - 1, pairs],
+                    send_sem=send_sem.at[g, d - 1],
+                    recv_sem=recv_sem.at[g, d - 1],
+                    device_id=(to * CORES + core, i),
                     device_id_type=MESH,
                 )
             )
         return copies
 
-    def transform(step):
+    def join(g):
+        pairs = pl.ds(*spans[g])
+        twin_copy(g).wait_recv()
+        joined[pairs] = stage[pairs, pl.ds(own_half, half_slots)] + recv_twin[pairs]
+        for copy in chip_copies(g):
+            copy.start()
+
+    def load(step):
         for k in range(per_step):
             vol_copy(step * per_step + k).wait()
         planes = pl.ds(step * per_step, per_step)
         near = vol[planes, :, pl.ds(0, box // 2)].reshape(per_step * n_row, box // 2)
         far = vol[planes, :, pl.ds(box // 2, box // 2)].reshape(per_step * n_row, box // 2)
-        inputs = (halves(near + far), halves(near - far))
-        if step == 0:
-            for copy in tab_copies:
-                copy.wait()
+        return halves(near + far), halves(near - far)
+
+    def transform(step, inputs, chunks):
         rows = pl.ds((step * per_step + 1) * n_row, per_step * n_row)
-        for cb in range(half_blocks):
+        for cb in chunks:
             xh, xl = inputs[cb % 2]
             at = pl.ds(cb * 2 * LANES, 2 * LANES)
             th, tl = t_high[:, at], t_low[:, at]
@@ -250,41 +284,55 @@
             z_high[rows, at] = zh
             z_low[rows, at] = zl
 
-    for step in range(n_plane // per_step):
-        if per_step <= 2:
-            given = [weights(step * per_step + k) for k in range(per_step)]
-            transform(step)
-            if step == 0:
-                pl.semaphore_wait(barrier, n_slab - 1 + n_img - 1)
+    for copy in tab_copies:
+        copy.wait()
+    given = None
+    few = per_step <= 2
+    for step in range(n_step + 1):
+        if step < n_step:
+            inputs = load(step)
+        ready = []
+        if few:
             for k in range(per_step):
-                pair = step * per_step + k
-                evaluate(pair, given[k])
-                for copy in sends(pair):
-                    copy.start()
+                if step < n_step:
+                    ready.append(weights(step * per_step + k))
+                    each = half_blocks // per_step
+                    transform(step, inputs, range(k * each, (k + 1) * each))
+                if step > 0:
+                    evaluate((step - 1) * per_step + k, given[k])
+            if step == n_step - 1:
+                ready.append(weights(n_plane))
+            if step == n_step:
+                evaluate(n_plane, given[per_step])
         else:
-            transform(step)
-            if step == 0:
-                pl.semaphore_wait(barrier, n_slab - 1 + n_img - 1)
-
-            def body(k, carry):
-                evaluate(k, weights(k))
-                for copy in sends(k):
-                    copy.start()
-                return carry
-
-            lax.fori_loop(step * per_step, (step + 1) * per_step, body, 0)
-    evaluate(n_plane, weights(n_plane))
-    for copy in sends(n_plane):
-        copy.start()
-
-    own = pl.ds(pl.multiple_of(s * tile, tile), tile)
-    for pair in range(n_pair):
-        pltpu.make_async_copy(recv.at[pair], recv.at[pair], recv_sem.at[pair]).wait()
-        total = stage[pair, own]
-        for d in range(n_slab - 1):
-            total = total + recv[pair, d]
-        for to in range(n_img):
-            red[to, pl.ds(MOST * pair, MOST)] = total[MOST * to : MOST * to + MOST]
+            if step < n_step:
+                transform(step, inputs, range(half_blocks))
+            if step > 0:
+
+                def body(k, carry):
+                    evaluate(k, weights(k))
+                    return carry
+
+                lax.fori_loop(spans[step - 1][0], sum(spans[step - 1]), body, 0)
+        given = ready
+        if step == 1:
+            pl.semaphore_wait(barrier, n_chip + n_img - 1)
+        if step > 0:
+            twin_copy(step - 1).start()
+        if step > 1:
+            join(step - 2)
+    join(n_step - 1)
+
+    own = pl.ds(pl.multiple_of(chip * tile, tile), tile)
+    for g in range(n_step):
+        for copy in chip_copies(g):
+            copy.wait_recv()
+        for pair in range(spans[g][0], sum(spans[g])):
+            total = joined[pair, own]
+            for d in range(n_chip - 1):
+                total = total + recv[d, pair]
+            for to in range(n_img):
+                red[to, pl.ds(MOST * pair, MOST)] = total[MOST * to : MOST * to + MOST]
 
     copies = []
     for d in range(1, n_img):
@@ -306,7 +354,8 @@
     group = s * n_img + i
     eye = lax.broadcasted_iota(jnp.int32, (n_blk, n_blk), 0) == lax.broadcasted_iota(jnp.int32, (n_blk, n_blk), 1)
     before = lax.broadcasted_iota(jnp.int32, (n_blk, n_blk), 1) < lax.broadcasted_iota(jnp.int32, (n_blk, n_blk), 0)
-    lines = [meta_ref[k, pl.ds(group * MOST, 1)] for k in range(6)]
+    own_line = core * half_slots + chip * tile + i * MOST
+    lines = [meta_ref[k, pl.ds(own_line, 1)] for k in range(6)]
     plane_b, row_b, col_b, _, _, focus_b = [
         jnp.sum(jnp.where(eye, v, 0.0), axis=1, keepdims=True) for v in lines
     ]
@@ -359,9 +408,10 @@
 
     for copy in copies:
         copy.wait_send()
-    for pair in range(n_pair):
-        some = stage.at[pair, pl.ds(0, (n_slab - 1) * tile)]
-        pltpu.make_async_copy(some, some, send_sem.at[pair]).wait()
+    for g in range(n_step):
+        twin_copy(g).wait_send()
+        for copy in chip_copies(g):
+            copy.wait_send()
 
 
 def on_device(n_slab, n_img, volume, blk_plane, blk_row, blk_col, frac_plane, frac_row, defocus):
@@ -373,6 +423,7 @@
     n_slot = MOST * n_group
     tile = MOST * n_img
     per_step = max(1, min(n_plane, 256 // n_row))
+    n_step = n_plane // per_step
     pad = -(-MOST * n_pair // 8) * 8
     table_high, table_low = column_table(box)
     dims = (n_slab, n_img, n_plane, n_row, box, n_group, n_blk, per_step)
@@ -394,14 +445,17 @@
             pltpu.VMEM(((n_plane + 2) * n_row, box), BF16),
             pltpu.VMEM(((n_plane + 2) * n_row, box), BF16),
             pltpu.VMEM((n_pair, n_slot, 2 * LANES), F32),
-            pltpu.VMEM((n_pair, n_slab - 1, tile, 2 * LANES), F32),
+            pltpu.VMEM((n_pair, n_slot // CORES, 2 * LANES), F32),
+            pltpu.VMEM((n_pair, n_slot // CORES, 2 * LANES), F32),
+            pltpu.VMEM((n_slab // CORES - 1, n_pair, tile, 2 * LANES), F32),
             pltpu.VMEM((n_img, pad, 2 * LANES), F32),
             pltpu.VMEM((n_img, pad, 2 * LANES), F32),
             pltpu.SemaphoreType.DMA((6,)),
             pltpu.SemaphoreType.DMA((n_plane,)),
             pltpu.SemaphoreType.DMA((2,)),
-            pltpu.SemaphoreType.DMA((n_pair,)),
-            pltpu.SemaphoreType.DMA((n_pair,)),
+            pltpu.SemaphoreType.DMA((2, n_step)),
+            pltpu.SemaphoreType.DMA((n_step, n_slab // CORES - 1)),
+            pltpu.SemaphoreType.DMA((n_step, n_slab // CORES - 1)),
             pltpu.SemaphoreType.DMA((n_img - 1,)),
             pltpu.SemaphoreType.DMA((n_img - 1,)),
         ],

time: 24.9 us -> 24.4 us (0.980)
  Pallas kernels: 23.3 us -> 22.8 us
    pallas_call x1, Pallas kernels: 23.3 us -> 22.8 us  [on_device(): pl.pallas_call(functools.partial(kernel, dims), out_shape=jax.ShapeDtypeS...]
where the time goes in v2:
time: 24.4 us; the launch traced here: 24.2 us
  Pallas kernels  22.8 us (93%)
  local copies, waits for them, and re-layouts  1.38 us (6%)
    pallas_call x1, Pallas kernels, on_device(): pl.pallas_call(functools.partial(kernel, dims), out_shape=jax.ShapeDtypeS...  22.8 us
    unnamed x1, local copies, waits for them, and re-layouts  1.38 us

profile of v2, /device:TPU:0, one launch (start us, length us, event | category | flops | bytes accessed | tf_op | source)
XLA Modules:
  0.0 24.2 jit_solution(2006593983886150413)
XLA Ops:
  0.0 22.8 %slices.1 = f32[32,2,128]{2,1,0:T(2,128)} custom-call(s32[8,128]{1,0:T(8,128)} %bitcast.8, s32[8,128]{1,0:T(8,128)} %bitcast.9, s32[8,128]{1,0:T(8,128)} %bitcast.10, f32[8,128]{1,0:T(8,128)} %bitcast.11, f32[8,128]{1,0:T(8,128)} %bitcast.12, f32[1,128]{1,0:T(1,128)} %bitcast.13, f32[8,128,1024]{2,1,0:T(8,128)} %vol_hbm.1, ...), custom_call_target="tpu_custom_call" | custom-call | flops 8000000000 | bytes 9000000 | tf_op jit(solution)/shard_map/slices/pallas_call | solution.py:432
  22.8 1.4 %copy.11 = f32[4,8,2,128]{3,2,1,0:T(2,128)} copy(f32[4,8,2,128]{3,2,1,0:T(2,128)} %bitcast.7) | data formatting | bytes 65536

commit v3 on v2

--- a/solution.py
+++ b/solution.py
@@ -14,10 +14,21 @@
 CTF_SCALE = 20.0
 CTF_PHASE = 0.07
 MOST = 2
+KEY = 8192.0
 CORES = 2
 MESH = pl.DeviceIdType.MESH
 F32 = jnp.float32
 BF16 = jnp.bfloat16
+
+
+def stacked(value):
+    return jnp.concatenate(halves(value), axis=0)
+
+
+def product(both, high, low):
+    rows = both.shape[0] // 2
+    wide = dot(both, high)
+    return wide[:rows] + wide[rows:] + dot(both[:rows], low)
 
 
 def wave_coefficients():
@@ -148,7 +159,16 @@
     slot_at = (slot_at // tile * CORES + slot_core) * n_img + slot_at % tile // MOST
     image_at = lax.broadcasted_iota(jnp.int32, (n_slot, n_image), 1) // own_images
     spread = jnp.where(slot_at == image_at, 1.0, 0.0)
-    sources = [ints[k].astype(F32) for k in range(3)] + [floats[0], floats[1]]
+    plane_of_block, row_of_block, col_of_block = [ints[k].astype(F32) for k in range(3)]
+    at_image = lax.broadcasted_iota(jnp.int32, (img_blk, n_image), 1) % own_images
+    seen = jnp.zeros((img_blk, n_image), F32)
+    for back in range(1, own_images):
+        earlier = pltpu.roll(plane_of_block, back, 1)
+        for turned in range(img_blk):
+            other = pltpu.roll(earlier, turned, 0) if turned else earlier
+            seen = jnp.where((at_image >= back) & (other == plane_of_block), 1.0, seen)
+    n_col = box // LANES
+    sources = [plane_of_block + KEY * seen, row_of_block * n_col + col_of_block, floats[0], floats[1]]
     sources.append(jnp.broadcast_to(focus_ref[...], (img_blk, n_image)))
     for k, source in enumerate(sources):
         laid = jnp.where(in_turn, jnp.concatenate([source] * own_images, axis=0), 0.0)
@@ -160,29 +180,25 @@
     lane = lax.broadcasted_iota(jnp.int32, (1, n_row), 1)
     y = (lane + s * n_row).astype(F32)
     step_cos, step_sin = wave(y * (1.0 / box))
-    blk = lax.broadcasted_iota(jnp.int32, (n_slot, n_blk), 1).astype(F32)
-    turn = lax.broadcasted_iota(jnp.int32, (n_slot, 1), 0) % MOST
+    turn = (lax.broadcasted_iota(jnp.int32, (n_slot, 1), 0) % MOST).astype(F32) * KEY
 
     def weights(pair):
-        plane = (n_plane * i - 1 + pair).astype(F32)
-        here = meta_ref[0] == plane
-        first = jnp.min(jnp.where(here, blk, 1e6), axis=1, keepdims=True)
-        last = jnp.max(jnp.where(here, blk, -1.0), axis=1, keepdims=True)
-        chosen = jnp.where(turn == 0, first, jnp.where(last > first, last, -2.0))
-        mask = blk == chosen
+        plane = n_plane * i - 1 + pair
+        mask = meta_ref[0] == turn + plane.astype(F32)
 
         def pick(k):
             return jnp.sum(jnp.where(mask, meta_ref[k], 0.0), axis=1, keepdims=True)
 
-        row, col, fz, fy = pick(1), pick(2), pick(3), pick(4)
+        code, fz, fy = pick(1), pick(2), pick(3)
+        row = jnp.floor(code * (1.0 / n_col))
+        col = code - row * n_col
         cosine, sine = wave(row * y * (1.0 / box))
         h_real = (1.0 - fy) + fy * step_cos
         h_imag = -fy * step_sin
         g_real = cosine * h_real + sine * h_imag
         g_imag = cosine * h_imag - sine * h_real
         both = [jnp.concatenate([part * (1.0 - fz), part * fz], axis=1) for part in (g_real, g_imag)]
-        high, low = halves(jnp.concatenate(both, axis=0))
-        return col, high, low
+        return col, stacked(jnp.concatenate(both, axis=0))
 
     slot_lane = lax.broadcasted_iota(jnp.int32, (n_slot, LANES), 1)
 
@@ -190,7 +206,7 @@
         rows = pl.ds(pair * n_row, 2 * n_row)
         if not isinstance(pair, int):
             rows = pl.ds(pl.multiple_of(pair * n_row, n_row), 2 * n_row)
-        col, gh, gl = given
+        col, rows_of = given
         mirrored = col >= float(half_blocks)
         base = jnp.where(mirrored, 2.0 * half_blocks - 1.0 - col, col)
         odd = base - 2.0 * jnp.floor(base * 0.5)
@@ -202,8 +218,7 @@
         real = imag = past_real = past_imag = None
         for cb in range(half_blocks):
             at = pl.ds(cb * 2 * LANES, 2 * LANES)
-            zh, zl = z_high[rows, at], z_low[rows, at]
-            prod = dot(gh, zh) + dot(gl, zh) + dot(gh, zl)
+            prod = product(rows_of, z_high[rows, at], z_low[rows, at])
             a, b = prod[:n_slot, :LANES], prod[:n_slot, LANES:]
             c, d = prod[n_slot:, :LANES], prod[n_slot:, LANES:]
             now_real, now_imag = a - sign * d, c + sign * b
@@ -271,15 +286,13 @@
         planes = pl.ds(step * per_step, per_step)
         near = vol[planes, :, pl.ds(0, box // 2)].reshape(per_step * n_row, box // 2)
         far = vol[planes, :, pl.ds(box // 2, box // 2)].reshape(per_step * n_row, box // 2)
-        return halves(near + far), halves(near - far)
+        return stacked(near + far), stacked(near - far)
 
     def transform(step, inputs, chunks):
         rows = pl.ds((step * per_step + 1) * n_row, per_step * n_row)
         for cb in chunks:
-            xh, xl = inputs[cb % 2]
             at = pl.ds(cb * 2 * LANES, 2 * LANES)
-            th, tl = t_high[:, at], t_low[:, at]
-            z = dot(xh, th) + dot(xl, th) + dot(xh, tl)
+            z = product(inputs[cb % 2], t_high[:, at], t_low[:, at])
             zh, zl = halves(z)
             z_high[rows, at] = zh
             z_low[rows, at] = zl
@@ -321,45 +334,13 @@
             twin_copy(step - 1).start()
         if step > 1:
             join(step - 2)
-    join(n_step - 1)
-
-    own = pl.ds(pl.multiple_of(chip * tile, tile), tile)
-    for g in range(n_step):
-        for copy in chip_copies(g):
-            copy.wait_recv()
-        for pair in range(spans[g][0], sum(spans[g])):
-            total = joined[pair, own]
-            for d in range(n_chip - 1):
-                total = total + recv[d, pair]
-            for to in range(n_img):
-                red[to, pl.ds(MOST * pair, MOST)] = total[MOST * to : MOST * to + MOST]
-
-    copies = []
-    for d in range(1, n_img):
-        to = lax.rem(i + d, n_img)
-        copies.append(
-            pltpu.make_async_remote_copy(
-                src_ref=red.at[to],
-                dst_ref=recv2.at[i],
-                send_sem=send2_sem.at[d - 1],
-                recv_sem=recv2_sem.at[d - 1],
-                device_id=(s, to),
-                device_id_type=MESH,
-            )
-        )
-    for copy in copies:
-        copy.start()
-    recv2[i] = red[i]
-
     group = s * n_img + i
     eye = lax.broadcasted_iota(jnp.int32, (n_blk, n_blk), 0) == lax.broadcasted_iota(jnp.int32, (n_blk, n_blk), 1)
-    before = lax.broadcasted_iota(jnp.int32, (n_blk, n_blk), 1) < lax.broadcasted_iota(jnp.int32, (n_blk, n_blk), 0)
     own_line = core * half_slots + chip * tile + i * MOST
-    lines = [meta_ref[k, pl.ds(own_line, 1)] for k in range(6)]
-    plane_b, row_b, col_b, _, _, focus_b = [
-        jnp.sum(jnp.where(eye, v, 0.0), axis=1, keepdims=True) for v in lines
-    ]
-    rank_b = jnp.sum(jnp.where(before & (lines[0] == plane_b), 1.0, 0.0), axis=1, keepdims=True)
+    lines = [meta_ref[k, pl.ds(own_line, 1)] for k in (0, 1, 4)]
+    key_b, code_b, focus_b = [jnp.sum(jnp.where(eye, v, 0.0), axis=1, keepdims=True) for v in lines]
+    row_b = jnp.floor(code_b * (1.0 / n_col))
+    col_b = code_b - row_b * n_col
     pad = red.shape[1]
     n_sum = n_img * pad
     place = lax.broadcasted_iota(jnp.int32, (n_blk, n_sum), 1)
@@ -367,9 +348,8 @@
     for k in range(1, n_img):
         img_of = img_of + jnp.where(place >= k * pad, 1, 0)
     rest = place - img_of * pad
-    plane_of = (img_of * n_plane - 1 + rest // MOST).astype(F32)
-    turn_of = (rest % MOST).astype(F32)
-    take = (rest < MOST * n_pair) & (plane_of == plane_b) & (turn_of == rank_b)
+    key_of = (img_of * n_plane - 1 + rest // MOST).astype(F32) + (rest % MOST).astype(F32) * KEY
+    take = (rest < MOST * n_pair) & (key_of == key_b)
     take = jnp.where(take, 1.0, 0.0).astype(BF16)
 
     lane_x = lax.broadcasted_iota(jnp.int32, (n_blk, LANES), 1).astype(F32)
@@ -392,6 +372,36 @@
     mirrored_b = col_b >= float(half_blocks)
     base_b = jnp.where(mirrored_b, 2.0 * half_blocks - 1.0 - col_b, col_b)
     odd_b = base_b - 2.0 * jnp.floor(base_b * 0.5) > 0.0
+
+    join(n_step - 1)
+
+    own = pl.ds(pl.multiple_of(chip * tile, tile), tile)
+    for g in range(n_step):
+        for copy in chip_copies(g):
+            copy.wait_recv()
+        for pair in range(spans[g][0], sum(spans[g])):
+            total = joined[pair, own]
+            for d in range(n_chip - 1):
+                total = total + recv[d, pair]
+            for to in range(n_img):
+                red[to, pl.ds(MOST * pair, MOST)] = total[MOST * to : MOST * to + MOST]
+
+    copies = []
+    for d in range(1, n_img):
+        to = lax.rem(i + d, n_img)
+        copies.append(
+            pltpu.make_async_remote_copy(
+                src_ref=red.at[to],
+                dst_ref=recv2.at[i],
+                send_sem=send2_sem.at[d - 1],
+                recv_sem=recv2_sem.at[d - 1],
+                device_id=(s, to),
+                device_id_type=MESH,
+            )
+        )
+    for copy in copies:
+        copy.start()
+    recv2[i] = red[i]
 
     for copy in copies:
         copy.wait_recv()
@@ -438,7 +448,7 @@
             pltpu.VMEM((3, img_blk, n_image), jnp.int32),
             pltpu.VMEM((2, img_blk, n_image), F32),
             pltpu.VMEM((1, n_image), F32),
-            pltpu.VMEM((6, n_slot, n_blk), F32),
+            pltpu.VMEM((5, n_slot, n_blk), F32),
             pltpu.VMEM((n_plane, n_row, box), F32),
             pltpu.VMEM((box // 2, box), BF16),
             pltpu.VMEM((box // 2, box), BF16),

time: 24.4 us -> 24.4 us (level)
  no operation moved by 1% of the time
where the time goes in v3:
time: 24.4 us; the launch traced here: 24.2 us
  Pallas kernels  22.8 us (93%)
  local copies, waits for them, and re-layouts  1.38 us (6%)
    pallas_call x1, Pallas kernels, on_device(): pl.pallas_call(functools.partial(kernel, dims), out_shape=jax.ShapeDtypeS...  22.8 us
    unnamed x1, local copies, waits for them, and re-layouts  1.38 us

profile of v3, /device:TPU:0, one launch (start us, length us, event | category | flops | bytes accessed | tf_op | source)
XLA Modules:
  0.0 24.2 jit_solution(18363789678353910921)
XLA Ops:
  0.0 22.8 %slices.1 = f32[32,2,128]{2,1,0:T(2,128)} custom-call(s32[8,128]{1,0:T(8,128)} %bitcast.8, s32[8,128]{1,0:T(8,128)} %bitcast.9, s32[8,128]{1,0:T(8,128)} %bitcast.10, f32[8,128]{1,0:T(8,128)} %bitcast.11, f32[8,128]{1,0:T(8,128)} %bitcast.12, f32[1,128]{1,0:T(1,128)} %bitcast.13, f32[8,128,1024]{2,1,0:T(8,128)} %vol_hbm.1, ...), custom_call_target="tpu_custom_call" | custom-call | flops 8000000000 | bytes 9000000 | tf_op jit(solution)/shard_map/slices/pallas_call | solution.py:442
  22.8 1.4 %copy.11 = f32[4,8,2,128]{3,2,1,0:T(2,128)} copy(f32[4,8,2,128]{3,2,1,0:T(2,128)} %bitcast.7) | data formatting | bytes 65536

commit v4 on v3

--- a/solution.py
+++ b/solution.py
@@ -129,8 +129,6 @@
     for q in range(per_step):
         vol_copy(q).start()
     tab_copies[1].start()
-    for q in range(per_step, n_plane):
-        vol_copy(q).start()
 
     barrier = pltpu.get_barrier_semaphore()
     pl.semaphore_signal(barrier, inc=1, device_id=(twin, i), device_id_type=MESH)
@@ -299,6 +297,8 @@
 
     for copy in tab_copies:
         copy.wait()
+    for q in range(per_step, n_plane):
+        vol_copy(q).start()
     given = None
     few = per_step <= 2
     for step in range(n_step + 1):

time: 24.4 us -> 23.8 us (0.975)
  Pallas kernels: 22.8 us -> 22.2 us
    pallas_call x1, Pallas kernels: 22.8 us -> 22.2 us  [on_device(): pl.pallas_call(functools.partial(kernel, dims), out_shape=jax.ShapeDtypeS...]
where the time goes in v4:
time: 23.8 us; the launch traced here: 23.6 us
  Pallas kernels  22.2 us (93%)
  local copies, waits for them, and re-layouts  1.38 us (6%)
    pallas_call x1, Pallas kernels, on_device(): pl.pallas_call(functools.partial(kernel, dims), out_shape=jax.ShapeDtypeS...  22.2 us
    unnamed x1, local copies, waits for them, and re-layouts  1.38 us

profile of v4, /device:TPU:0, one launch (start us, length us, event | category | flops | bytes accessed | tf_op | source)
XLA Modules:
  0.0 23.6 jit_solution(2307736296505499650)
XLA Ops:
  0.0 22.2 %slices.1 = f32[32,2,128]{2,1,0:T(2,128)} custom-call(s32[8,128]{1,0:T(8,128)} %bitcast.8, s32[8,128]{1,0:T(8,128)} %bitcast.9, s32[8,128]{1,0:T(8,128)} %bitcast.10, f32[8,128]{1,0:T(8,128)} %bitcast.11, f32[8,128]{1,0:T(8,128)} %bitcast.12, f32[1,128]{1,0:T(1,128)} %bitcast.13, f32[8,128,1024]{2,1,0:T(8,128)} %vol_hbm.1, ...), custom_call_target="tpu_custom_call" | custom-call | flops 8000000000 | bytes 9000000 | tf_op jit(solution)/shard_map/slices/pallas_call | solution.py:442
  22.2 1.4 %copy.11 = f32[4,8,2,128]{3,2,1,0:T(2,128)} copy(f32[4,8,2,128]{3,2,1,0:T(2,128)} %bitcast.7) | data formatting | bytes 65536
